TPU v7x, 32 devices: a whole 2x2x4 slice. The times are simulated.
32 devices in a mesh: row: 4 (over y, x), col: 8 (over z, core).
Axes of the slice: x: 2, y: 2, z: 4, core: 2. Of those that a mesh axis runs over, the one named last changes fastest.
Arguments:
- tokens: bfloat16 [16384, 1024], P(('row', 'col')), may hold values from -6 to 6
- gain_attn: bfloat16 [1024], P(('row', 'col')), may hold values from 0.099609375 to 1.8984375
- w_query: bfloat16 [1024, 1024], P(('row', 'col')), may hold values from -0.1875 to 0.1875
- w_keyval: bfloat16 [1024, 256], P(('row', 'col')), may hold values from -0.1875 to 0.1875
- w_out: bfloat16 [1024, 1024], P(('row', 'col')), may hold values from -3 to 3
- gain_mlp: bfloat16 [1024], P(('row', 'col')), may hold values from 0.099609375 to 1.8984375
- w_gate: bfloat16 [1024, 3072], P('row', 'col'), may hold values from -0.1875 to 0.1875
- w_up: bfloat16 [1024, 3072], P('row', 'col'), may hold values from -0.1875 to 0.1875
- w_down: bfloat16 [3072, 1024], P('col', 'row'), may hold values from -0.109375 to 0.109375
- segment: int32 [16384], P(('row', 'col')), may hold values from 0 to 15, as said below
- cotangent: bfloat16 [16384, 1024], P(('row', 'col')), may hold values from -6 to 6
Outputs:
- output: bfloat16 [16384, 1024], P(('row', 'col'))
- grad_tokens: float32 [16384, 1024], P(('row', 'col'))
- grad_gain_attn: float32 [1024], P(('row', 'col'))
- grad_query: float32 [1024, 1024], P(('row', 'col'))
- grad_keyval: float32 [1024, 256], P(('row', 'col'))
- grad_out: float32 [1024, 1024], P(('row', 'col'))
- grad_gain_mlp: float32 [1024], P(('row', 'col'))
- grad_gate: float32 [1024, 3072], P('row', 'col')
- grad_up: float32 [1024, 3072], P('row', 'col')
- grad_down: float32 [3072, 1024], P('col', 'row')
Inputs may be any that keep to these rules, and one draw needn't show every extreme that they name: `segment`: never falling; each pack of 2048 tokens holds two documents, numbered 2p and 2p + 1 for pack p; the first one is 512 to 1536 tokens long.
All inputs are finite; a program needn't handle non-finite values.
Results may differ from a plain program's by a relative error of at most 0.014.
Values may be sent and summed in bfloat16 or wider, within the bound.
A program may use at most 256 MiB of HBM per device.

v0:
```python
import math

import jax
import jax.numpy as jnp
from jax import lax
from jax.sharding import PartitionSpec as P

H = 8
DH = 128
WINDOW = 1024


EPS = 1e-06
NEGATIVE = -1e30


def from_behind(block, axis, distance):
    devices = range(lax.axis_size(axis))
    route = [(i - distance, i) for i in devices if i - distance in devices]
    return lax.ppermute(block, axis, route)


def product(left, right):
    return jnp.dot(left, right, preferred_element_type=jnp.float32)


def inner(left, right):
    return lax.dot_general(
        left, right, (((0,), (0,)), ((), ())), preferred_element_type=jnp.float32
    )


def against(left, right):
    return lax.dot_general(
        left, right, (((1,), (1,)), ((), ())), preferred_element_type=jnp.float32
    )


def gated(gate, up):
    return jax.nn.gelu(gate, approximate=True) * up


def norm_back(grad_normed, value, scale):
    return scale * grad_normed - value * scale**3 * jnp.mean(
        grad_normed * value, axis=-1, keepdims=True
    )


def shards(
    tokens, gain_attn, w_query, w_keyval, w_out, gain_mlp, w_gate, w_up, w_down, segment, cotangent
):
    gain_first, gain_second, query_weight, keyval_weight, out_weight = (
        lax.all_gather(gain_attn, ("row", "col"), axis=0, tiled=True),
        lax.all_gather(gain_mlp, ("row", "col"), axis=0, tiled=True),
        lax.all_gather(w_query, ("row", "col"), axis=0, tiled=True),
        lax.all_gather(w_keyval, ("row", "col"), axis=0, tiled=True),
        lax.all_gather(w_out, ("row", "col"), axis=0, tiled=True),
    )
    gain_first = gain_first.astype(jnp.float32)
    gain_second = gain_second.astype(jnp.float32)
    rows = tokens.shape[0]
    inputs = tokens.astype(jnp.float32)
    scale_first = lax.rsqrt(jnp.mean(inputs * inputs, axis=-1, keepdims=True) + EPS)
    normed_first = inputs * scale_first
    attn_in = (normed_first * gain_first).astype(jnp.bfloat16)
    query = product(attn_in, query_weight).astype(jnp.bfloat16)
    keyval = product(attn_in, keyval_weight).astype(jnp.bfloat16)
    marks = segment + 1
    reach = (WINDOW + rows - 2) // rows
    pieces = [keyval]
    piece_marks = [marks]
    for offset in range(1, reach + 1):
        moved, moved_marks = from_behind((keyval, marks), "col", offset)
        pieces.insert(0, moved)
        piece_marks.insert(0, moved_marks)
    keys_all = jnp.concatenate(pieces, axis=0)
    marks_all = jnp.concatenate(piece_marks, axis=0)
    keys = keys_all[:, :DH]
    values = keys_all[:, DH:]
    query_places = reach * rows + jnp.arange(rows, dtype=jnp.int32)
    key_places = jnp.arange(keys_all.shape[0], dtype=jnp.int32)
    gap = query_places[:, None] - key_places[None, :]
    allowed = (marks[:, None] == marks_all[None, :]) & (gap >= 0) & (gap < WINDOW)
    group = min(H, max(1, 1024 // rows))
    blocks = H // group
    scale = 1.0 / math.sqrt(DH)
    query_groups = query.reshape(rows, blocks, group, DH).transpose(1, 2, 0, 3)

    def scores_of(part):
        scores = jnp.einsum("gqd,kd->gqk", part, keys, preferred_element_type=jnp.float32) * scale
        return jnp.where(allowed[None], scores, NEGATIVE)

    def forward_group(part):
        scores = scores_of(part)
        top = jnp.max(scores, axis=-1, keepdims=True)
        expo = jnp.where(allowed[None], jnp.exp(scores - top), 0.0)
        total = jnp.sum(expo, axis=-1, keepdims=True)
        probs = expo / total
        mixed = jnp.einsum(
            "gqk,kd->gqd", probs.astype(jnp.bfloat16), values, preferred_element_type=jnp.float32
        )
        return (mixed.astype(jnp.bfloat16), top + jnp.log(total))

    mixed_groups, logsum = lax.map(forward_group, query_groups)
    attended = mixed_groups.transpose(2, 0, 1, 3).reshape(rows, H * DH)
    middle = inputs + product(attended, out_weight)
    scale_second = lax.rsqrt(jnp.mean(middle * middle, axis=-1, keepdims=True) + EPS)
    normed_second = middle * scale_second
    mlp_in = (normed_second * gain_second).astype(jnp.bfloat16)
    gate_weight, up_weight, down_weight = (
        lax.all_gather(w_gate, "row", axis=0, tiled=True),
        lax.all_gather(w_up, "row", axis=0, tiled=True),
        lax.all_gather(w_down, "row", axis=1, tiled=True),
    )
    piece = lax.all_gather(mlp_in, "col", axis=0, tiled=True)
    hidden = gated(product(piece, gate_weight), product(piece, up_weight)).astype(jnp.bfloat16)
    mlp_out = lax.psum_scatter(
        product(hidden, down_weight).astype(jnp.bfloat16), "col", scatter_dimension=0, tiled=True
    ).astype(jnp.float32)
    output = (middle + mlp_out).astype(jnp.bfloat16)
    inputs_piece = lax.all_gather(mlp_in, "col", axis=0, tiled=True)
    grad_piece = lax.all_gather(cotangent, "col", axis=0, tiled=True)
    gate_rows = product(inputs_piece, gate_weight)
    up_rows = product(inputs_piece, up_weight)
    grad_hidden = against(grad_piece, down_weight)
    _, pull = jax.vjp(gated, gate_rows, up_rows)
    grad_gate, grad_up = pull(grad_hidden)
    grad_gate = grad_gate.astype(jnp.bfloat16)
    grad_up = grad_up.astype(jnp.bfloat16)
    gate_grad = inner(inputs_piece, grad_gate)
    up_grad = inner(inputs_piece, grad_up)
    down_grad = inner(hidden, grad_piece)
    grad_mlp_in = lax.psum_scatter(
        against(grad_gate, gate_weight) + against(grad_up, up_weight),
        "col",
        scatter_dimension=0,
        tiled=True,
    )
    gate_grad, up_grad, down_grad = (
        lax.psum_scatter(
            gate_grad.astype(jnp.bfloat16), "row", scatter_dimension=0, tiled=True
        ).astype(jnp.float32),
        lax.psum_scatter(
            up_grad.astype(jnp.bfloat16), "row", scatter_dimension=0, tiled=True
        ).astype(jnp.float32),
        lax.psum_scatter(
            down_grad.astype(jnp.bfloat16), "row", scatter_dimension=1, tiled=True
        ).astype(jnp.float32),
    )
    grad_outputs = cotangent.astype(jnp.float32)
    gain_second_grad = jnp.sum(grad_mlp_in * normed_second, axis=0)
    grad_middle = grad_outputs + norm_back(grad_mlp_in * gain_second, middle, scale_second)
    grad_branch = grad_middle.astype(jnp.bfloat16)
    out_grad = inner(attended, grad_branch)
    grad_attended = against(grad_branch, out_weight).astype(jnp.bfloat16)
    grad_groups = grad_attended.reshape(rows, blocks, group, DH).transpose(1, 2, 0, 3)

    def backward_group(item):
        part, grad_part, logs = item
        scores = scores_of(part)
        probs = jnp.where(allowed[None], jnp.exp(scores - logs), 0.0)
        grad_probs = jnp.einsum(
            "gqd,kd->gqk", grad_part, values, preferred_element_type=jnp.float32
        )
        centre = jnp.sum(probs * grad_probs, axis=-1, keepdims=True)
        grad_scores = (probs * (grad_probs - centre)).astype(jnp.bfloat16)
        grad_part_query = (
            jnp.einsum("gqk,kd->gqd", grad_scores, keys, preferred_element_type=jnp.float32) * scale
        )
        grad_keys = (
            jnp.einsum("gqk,gqd->kd", grad_scores, part, preferred_element_type=jnp.float32) * scale
        )
        grad_values = jnp.einsum(
            "gqk,gqd->kd", probs.astype(jnp.bfloat16), grad_part, preferred_element_type=jnp.float32
        )
        return (grad_part_query, grad_keys, grad_values)

    query_parts, key_parts, value_parts = lax.map(
        backward_group, (query_groups, grad_groups, logsum)
    )
    grad_query_act = query_parts.transpose(2, 0, 1, 3).reshape(rows, H * DH).astype(jnp.bfloat16)
    grad_keyval_all = jnp.concatenate(
        [jnp.sum(key_parts, axis=0), jnp.sum(value_parts, axis=0)], axis=1
    )
    grad_own = grad_keyval_all[reach * rows :]
    for offset in range(1, reach + 1):
        sent = grad_keyval_all[(reach - offset) * rows : (reach - offset + 1) * rows]
        grad_own = grad_own + from_behind(sent.astype(jnp.bfloat16), "col", -offset).astype(
            sent.dtype
        )
    grad_keyval_act = grad_own.astype(jnp.bfloat16)
    grad_attn_in = against(grad_query_act, query_weight) + against(grad_keyval_act, keyval_weight)
    query_grad = inner(attn_in, grad_query_act)
    keyval_grad = inner(attn_in, grad_keyval_act)
    gain_first_grad = jnp.sum(grad_attn_in * normed_first, axis=0)
    grad_inputs = grad_middle + norm_back(grad_attn_in * gain_first, inputs, scale_first)
    gain_first_grad, gain_second_grad, query_grad, keyval_grad, out_grad = (
        lax.psum_scatter(gain_first_grad, ("row", "col"), scatter_dimension=0, tiled=True),
        lax.psum_scatter(gain_second_grad, ("row", "col"), scatter_dimension=0, tiled=True),
        lax.psum_scatter(query_grad, ("row", "col"), scatter_dimension=0, tiled=True),
        lax.psum_scatter(keyval_grad, ("row", "col"), scatter_dimension=0, tiled=True),
        lax.psum_scatter(out_grad, ("row", "col"), scatter_dimension=0, tiled=True),
    )
    return (
        output,
        grad_inputs,
        gain_first_grad,
        query_grad,
        keyval_grad,
        out_grad,
        gain_second_grad,
        gate_grad,
        up_grad,
        down_grad,
    )


def solution(mesh):
    return jax.shard_map(
        shards,
        mesh=mesh,
        in_specs=(
            P(("row", "col"), None),
            P(("row", "col")),
            P(("row", "col"), None),
            P(("row", "col"), None),
            P(("row", "col"), None),
            P(("row", "col")),
            P("row", "col"),
            P("row", "col"),
            P("col", "row"),
            P(("row", "col")),
            P(("row", "col"), None),
        ),
        out_specs=(
            P(("row", "col"), None),
            P(("row", "col"), None),
            P(("row", "col")),
            P(("row", "col"), None),
            P(("row", "col"), None),
            P(("row", "col"), None),
            P(("row", "col")),
            P("row", "col"),
            P("row", "col"),
            P("col", "row"),
        ),
        check_vma=False,
    )
```

profile of v0, /device:TPU:0, one launch (start us, length us, event | category | flops | bytes accessed | tf_op | source)
XLA Modules:
  0.0 1146.1 jit_solution(10954097477714334878)
XLA Ops:
  9.7 42.0 %all-reduce.5 = (bf16[1024]{0:T(1024)(128)(2,1)S(1)}, bf16[1024]{0:T(1024)(128)(2,1)S(1)}) all-reduce(bf16[1024]{0:T(1024)(128)(2,1)S(1)} %dynamic-update-slice, bf16[1024]{0:T(1024)(128)(2,1)S(1)} %dynamic-update-slice.1), channel_id=1, replica_groups=mesh['row'=4,'col'=8] {'row','col'}, use_global_device_ids=true, to_apply=%add | all-reduce | flops 2048 | bytes 8192
  53.8 43.2 %all_gather.33 = bf16[1024,256]{1,0:T(8,128)(2,1)S(1)} all-gather(bf16[32,256]{1,0:T(8,128)(2,1)} %param.18), channel_id=1, replica_groups=mesh['row'=4,'col'=8] {'row','col'}, dimensions={0}, use_global_device_ids=true | all-gather | bytes 540672 | tf_op jit(solution)/shard_map/all_gather | solution.py:56
  120.5 37.9 %while.28 = (s32[]{:T(128)}, bf16[4,2,512,128]{2,3,1,0:T(8,128)(2,1)S(1)}, f32[4,2,512,1]{2,1,3,0:T(2,128)}, bf16[4,2,512,128]{3,2,1,0:T(8,128)(2,1)}, bf16[1536...) while((s32[]{:T(128)}, ...), condition=%wide.region_4.5_spmd.clone, body=%wide.region_1.4_spmd.clone.sunk | while | flops 832175104 | bytes 24422520 | solution.py:104
  166.6 12.9 %all_gather.37 = bf16[1024,384]{1,0:T(8,128)(2,1)} all-gather(bf16[256,384]{1,0:T(8,128)(2,1)S(1)} %copy-done.16), channel_id=1, replica_groups=mesh['row'=4,'col'=8] {'row'}, dimensions={0}, use_global_device_ids=true | all-gather | bytes 983040 | tf_op jit(solution)/shard_map/all_gather | solution.py:111
  179.5 11.1 all_gather.38
  190.7 15.9 %all_gather.39 = bf16[384,1024]{1,0:T(8,128)(2,1)} all-gather(bf16[384,256]{1,0:T(8,128)(2,1)} %param.23), channel_id=1, replica_groups=mesh['row'=4,'col'=8] {'row'}, dimensions={1}, use_global_device_ids=true | all-gather | bytes 983040 | tf_op jit(solution)/shard_map/all_gather | solution.py:113
  206.6 40.5 %all-gather.9.cloned.1.call-done = bf16[4096,1024]{1,0:T(8,128)(2,1)} async-done(((bf16[512,1024]{1,0:T(8,128)(2,1)}), bf16[4096,1024]{1,0:T(8,128)(2,1)}) %all-gather.9.cloned.1.call-update) | async-done | bytes 8388624 | tf_op jit(solution)/shard_map/all_gather | solution.py:115
  247.1 9.8 fusion.87
  263.2 65.9 %all-gather.11.cloned.1.call-done = bf16[4096,1024]{1,0:T(8,128)(2,1)} async-done(((bf16[512,1024]{1,0:T(8,128)(2,1)}), bf16[4096,1024]{1,0:T(8,128)(2,1)}) %all-gather.11.cloned.1.call-update) | async-done | bytes 8388624 | tf_op jit(solution)/shard_map/all_gather | solution.py:122
  329.1 15.6 %multiply_convert_fusion.1 = (bf16[4096,384]{1,0:T(8,128)(2,1)S(1)}, bf16[4096,384]{1,0:T(8,128)(2,1)S(1)}, bf16[4096,384]{1,0:T(8,128)(2,1)}) fusion(f32[4096,384]{1,0:T(8,128)} %fusion.86, f32[4096,384]{1,0:T(8,128)} %fusion.87, bf16[4096,1024]{1,0:T(8,128)(2,1)} %all-gather.11.cloned.1.call-done, bf16[384,1024]{1,0:T(8,128)(2,1)} %all_gather.39), kind=kOutput, calls=%fused_computation.73 | convolution fusion | flops 3262119936 | bytes 31195136 | tf_op jit(solution)/shard_map/dot_general | solution.py:34
  344.8 8.2 fusion.88
  353.0 21.4 %convolution_add_fusion = f32[4096,1024]{1,0:T(8,128)} fusion(f32[4096,1024]{1,0:T(8,128)} %fusion.88, bf16[4096,384]{1,0:T(8,128)(2,1)S(1)} %get-tuple-element.213, bf16[1024,384]{1,0:T(8,128)(2,1)S(1)} %all_gather.38), kind=kOutput, calls=%fused_computation.64 | convolution fusion | flops 3225419776 | bytes 37486592 | tf_op jit(solution)/shard_map/dot_general | solution.py:34
  375.5 8.7 convolution_convert_fusion
  384.2 8.8 convolution_convert_fusion.3
  393.1 9.8 convolution_convert_fusion.4
  403.0 9.8 convolution_convert_fusion.5
  413.1 128.3 %reduce-scatter.11.cloned.1.call-done = f32[512,1024]{1,0:T(8,128)} async-done(((f32[4096,1024]{1,0:T(8,128)}), f32[512,1024]{1,0:T(8,128)}) %reduce-scatter.11.cloned.1.call-update) | async-done | bytes 2097168 | tf_op jit(solution)/shard_map/reduce_scatter | solution.py:133
  544.6 86.8 %reduce-scatter.9.cloned.1.call-done = bf16[512,1024]{1,0:T(8,128)(2,1)} async-done(((bf16[4096,1024]{1,0:T(8,128)(2,1)}), bf16[512,1024]{1,0:T(8,128)(2,1)}) %reduce-scatter.9.cloned.1.call-update) | async-done | bytes 1048592 | tf_op jit(solution)/shard_map/reduce_scatter | solution.py:117
  638.7 61.7 %while.29 = (s32[]{:T(128)}, bf16[4,2,512,128]{2,3,1,0:T(8,128)(2,1)}, f32[4,1536,128]{2,1,0:T(8,128)}, f32[4,1536,128]{2,1,0:T(8,128)}, bf16[4,2,512,128]{3,2,1...) while((s32[]{:T(128)}, ...), condition=%wide.region_11.12_spmd.clone, body=%wide.region_9.11_spmd.clone.sunk | while | flops 2034170880 | bytes 53903508 | solution.py:178
  708.8 8.9 collective-permute-done.5
  740.7 39.6 %all-reduce.4 = (f32[1024]{0:T(1024)S(1)}, f32[1024]{0:T(1024)S(1)}) all-reduce(f32[1024]{0:T(1024)S(1)} %get-tuple-element.161, f32[1024]{0:T(1024)S(1)} %copy-done.24), channel_id=4, replica_groups=mesh['row'=4,'col'=8] {'row','col'}, use_global_device_ids=true, to_apply=%region_16.17.clone | all-reduce | flops 2048 | bytes 16384
  784.9 70.1 %reduce-scatter.15.cloned.1.call-done = f32[32,256]{1,0:T(8,128)} async-done(((f32[1024,256]{1,0:T(8,128)}), f32[32,256]{1,0:T(8,128)}) %reduce-scatter.15.cloned.1.call-update) | async-done | bytes 32784 | tf_op jit(solution)/shard_map/reduce_scatter | solution.py:201
  855.0 141.9 %reduce-scatter.17.cloned.1.call-done = f32[32,1024]{1,0:T(8,128)} async-done(((f32[1024,1024]{1,0:T(8,128)}), f32[32,1024]{1,0:T(8,128)}) %reduce-scatter.17.cloned.1.call-update) | async-done | bytes 131088 | tf_op jit(solution)/shard_map/reduce_scatter | solution.py:202
  996.9 141.9 %reduce-scatter.13.cloned.1.call-done = f32[32,1024]{1,0:T(8,128)} async-done(((f32[1024,1024]{1,0:T(8,128)}), f32[32,1024]{1,0:T(8,128)}) %reduce-scatter.13.cloned.1.call-update) | async-done | bytes 131088 | tf_op jit(solution)/shard_map/reduce_scatter | solution.py:200
  (213 shorter events, 189.6 us)
Async XLA Ops:
  7.2 96.6 %copy-start.26 = (s32[512]{0:T(512)S(1)}, s32[512]{0:T(512)}, u32[]{:S(2)}) copy-start(s32[512]{0:T(512)} %param.24) | copy-start | bytes 6148
  7.2 104.5 %all-gather.5.cloned.1.call-start = ((), (), s32[]{:S(2)}) async-start(), calls=%async_computation.8 | async-start | bytes 2162688 | tf_op jit(solution)/shard_map/all_gather | solution.py:55
  7.9 152.9 %all-gather.7.cloned.1.call-start = ((), (), s32[]{:S(2)}) async-start(), calls=%async_computation.9 | async-start | bytes 2162688 | tf_op jit(solution)/shard_map/all_gather | solution.py:57
  51.7 55.4 %copy-start.19 = (f32[1024]{0:T(1024)}, f32[1024]{0:T(1024)S(1)}, u32[]{:S(2)}) copy-start(f32[1024]{0:T(1024)S(1)} %convert_element_type.99) | copy-start | bytes 12292
  53.8 53.2 %copy-start.22 = (f32[512]{0:T(512)}, f32[512]{0:T(512)S(1)}, u32[]{:S(2)}) copy-start(f32[512]{0:T(512)S(1)} %get-tuple-element.223) | copy-start | bytes 6148
  99.5 10.4 collective-permute-start.3
  101.8 8.1 collective-permute-start.2
  103.8 3.9 collective-permute-start.1
  105.7 4.2 collective-permute-start
  107.0 140.1 %all-gather.9.cloned.1.call-start = ((), (), s32[]{:S(2)}) async-start(), calls=%async_computation.10 | async-start | bytes 9437184 | tf_op jit(solution)/shard_map/all_gather | solution.py:115
  164.8 25.9 %copy-start.21 = (f32[512]{0:T(512)}, f32[512]{0:T(512)S(1)}, u32[]{:S(2)}) copy-start(f32[512]{0:T(512)S(1)} %get-tuple-element.225) | copy-start | bytes 6148
  166.0 163.1 %all-gather.11.cloned.1.call-start = ((), (), s32[]{:S(2)}) async-start(), calls=%async_computation.12 | async-start | bytes 9437184 | tf_op jit(solution)/shard_map/all_gather | solution.py:122
  166.6 374.8 %reduce-scatter.11.cloned.1.call-start = ((), (), s32[]{:S(2)}) async-start(), calls=%async_computation.13 | async-start | bytes 18874368 | tf_op jit(solution)/shard_map/reduce_scatter | solution.py:133
  374.4 257.1 %reduce-scatter.9.cloned.1.call-start = ((), (), s32[]{:S(2)}) async-start(), calls=%async_computation.11 | async-start | bytes 9437184 | tf_op jit(solution)/shard_map/reduce_scatter | solution.py:117
  384.2 345.9 %reduce-scatter.23.cloned.1.call-start = ((), (), s32[]{:S(2)}) async-start(), calls=%async_computation.19 | async-start | bytes 983040 | tf_op jit(solution)/shard_map/reduce_scatter | solution.py:146
  393.0 338.8 %reduce-scatter.21.cloned.1.call-start = ((), (), s32[]{:S(2)}) async-start(), calls=%async_computation.18 | async-start | bytes 983040 | tf_op jit(solution)/shard_map/reduce_scatter | solution.py:143
  402.9 330.7 %reduce-scatter.19.cloned.1.call-start = ((), (), s32[]{:S(2)}) async-start(), calls=%async_computation.17 | async-start | bytes 983040 | tf_op jit(solution)/shard_map/reduce_scatter | solution.py:140
  412.8 218.7 %copy-start.8 = (bf16[512,1024]{1,0:T(8,128)(2,1)S(1)}, bf16[512,1024]{1,0:T(8,128)(2,1)}, u32[]{:S(2)}) copy-start(bf16[512,1024]{1,0:T(8,128)(2,1)} %param.25) | copy-start | bytes 3145732
  412.8 442.2 %reduce-scatter.15.cloned.1.call-start = ((), (), s32[]{:S(2)}) async-start(), calls=%async_computation.15 | async-start | bytes 1081344 | tf_op jit(solution)/shard_map/reduce_scatter | solution.py:201
  705.2 3.6 collective-permute-start.4
  706.7 11.0 collective-permute-start.5
  720.6 276.4 %reduce-scatter.17.cloned.1.call-start = ((), (), s32[]{:S(2)}) async-start(), calls=%async_computation.16 | async-start | bytes 4325376 | tf_op jit(solution)/shard_map/reduce_scatter | solution.py:202
  725.3 413.5 %reduce-scatter.13.cloned.1.call-start = ((), (), s32[]{:S(2)}) async-start(), calls=%async_computation.14 | async-start | bytes 4325376 | tf_op jit(solution)/shard_map/reduce_scatter | solution.py:200
  738.5 42.9 %copy-start.25 = (f32[512]{0:T(512)S(1)}, f32[512]{0:T(512)}, u32[]{:S(2)}) copy-start(f32[512]{0:T(512)} %get-tuple-element.222) | copy-start | bytes 6148
  (22 other events, 164.0 us)
Sparse Core Ops, SparseCore 0:
  11.0 59.5 all-gather.4
  107.1 53.6 all-gather.6
  166.1 80.8 all-gather.8
  248.5 80.5 all-gather.10
  374.5 166.7 reduce-scatter.10
  543.5 87.9 reduce-scatter.8
  634.3 24.4 reduce-scatter.22
  661.7 26.0 reduce-scatter.20
  690.8 26.0 reduce-scatter.18
  720.7 134.2 reduce-scatter.14
  858.0 138.9 reduce-scatter.16
  999.7 139.0 reduce-scatter.12
where the time goes:
time: 1160 us; the launch traced here: 1150 us
  waiting for transfers between devices  691 us (60%)
  matrix products  193 us (17%)
  blocking collectives  165 us (14%)
  other arithmetic  50.9 us (4%)
  local copies, waits for them, and re-layouts  19.7 us (2%)
  between operations  15.1 us (1%)
    reduce_scatter x1, waiting for transfers between devices, shards(): lax.psum_scatter(out_grad, ('row', 'col'), scatter_dimension=0, tiled=True)  142 us
    reduce_scatter x1, waiting for transfers between devices, shards(): lax.psum_scatter(query_grad, ('row', 'col'), scatter_dimension=0, tiled=T...  142 us
    reduce_scatter x1, waiting for transfers between devices, shards(): lax.psum_scatter(against(grad_gate, gate_weight) + against(grad_up, up_we...  128 us
    reduce_scatter x1, waiting for transfers between devices, shards(): lax.psum_scatter(product(hidden, down_weight).astype(jnp.bfloat16), 'col'...  86.8 us
    unnamed x2, blocking collectives  81.6 us
    reduce_scatter x1, waiting for transfers between devices, shards(): lax.psum_scatter(keyval_grad, ('row', 'col'), scatter_dimension=0, tiled=...  70.1 us
    all_gather x1, waiting for transfers between devices, shards(): grad_piece = lax.all_gather(cotangent, 'col', axis=0, tiled=True)  65.9 us
    dot_general x6, matrix products, against(): lax.dot_general(left, right, (((1,), (1,)), ((), ())), preferred_element_...  51.9 us
  transfers between devices with their start and end apart: 18, of which 11 were waited for; matrix products, arithmetic and copies ran while one was open for 18% of the time, Pallas kernels for 0%

commit v1 on v0

--- a/solution.py
+++ b/solution.py
@@ -1,17 +1,466 @@
+import functools
 import math
 
 import jax
 import jax.numpy as jnp
 from jax import lax
+from jax.experimental import pallas as pl
+from jax.experimental.pallas import tpu as pltpu
 from jax.sharding import PartitionSpec as P
 
 H = 8
 DH = 128
 WINDOW = 1024
 
-
 EPS = 1e-06
 NEGATIVE = -1e30
+MESH = pl.DeviceIdType.MESH
+BF = jnp.bfloat16
+F32 = jnp.float32
+
+
+def product(left, right):
+    return jnp.dot(left, right, preferred_element_type=jnp.float32)
+
+
+def inner(left, right):
+    return lax.dot_general(
+        left, right, (((0,), (0,)), ((), ())), preferred_element_type=jnp.float32
+    )
+
+
+def against(left, right):
+    return lax.dot_general(
+        left, right, (((1,), (1,)), ((), ())), preferred_element_type=jnp.float32
+    )
+
+
+class Place:
+    def __init__(self, shape):
+        rows, cols = shape
+        self.X = math.isqrt(rows)
+        while rows % self.X:
+            self.X -= 1
+        self.Y = rows // self.X
+        self.Z = cols // 2
+        self.R = rows
+        self.row, self.col = lax.axis_index("row"), lax.axis_index("col")
+        self.y, self.x = self.row // self.X, self.row % self.X
+        self.z, self.core = self.col // 2, self.col % 2
+        self.xs, self.ys, self.zs = range(1, self.X), range(1, self.Y), range(1, self.Z)
+
+    def row_at(self, dy=0, dx=0):
+        return lax.rem(self.y + dy + self.Y, self.Y) * self.X + lax.rem(
+            self.x + dx + self.X, self.X
+        )
+
+    def z_at(self, dz):
+        return lax.rem(self.z + dz + self.Z, self.Z)
+
+    def device(self, dy=0, dx=0, dz=0, other=False):
+        core = 1 - self.core if other else self.core
+        return (self.row_at(dy, dx), self.z_at(dz) * 2 + core)
+
+    def greet(self):
+        barrier = pltpu.get_barrier_semaphore()
+        mates = [self.device(dx=d) for d in self.xs]
+        mates += [self.device(dy=d) for d in self.ys]
+        mates += [self.device(dz=d) for d in self.zs]
+        mates.append(self.device(other=True))
+        for mate in mates:
+            pl.semaphore_signal(barrier, inc=1, device_id=mate, device_id_type=MESH)
+        pl.semaphore_wait(barrier, len(mates))
+
+
+def remote(src, dst, send, recv, device):
+    return pltpu.make_async_remote_copy(
+        src_ref=src, dst_ref=dst, send_sem=send, recv_sem=recv, device_id=device,
+        device_id_type=MESH,
+    )
+
+
+class Sems:
+    def __init__(self, send, recv):
+        self.send, self.recv, self.count = send, recv, 0
+
+    def take(self):
+        self.count += 1
+        return self.send.at[self.count - 1], self.recv.at[self.count - 1]
+
+
+def gather_count(X, Y, Z):
+    return (Z - 1) + Z * ((X - 1) + (Y - 1) + 2 * (X - 1) * (Y - 1))
+
+
+class Gather:
+    def __init__(self, at, here, sems, own):
+        self.at, self.p, self.own = at, here, own
+        self.sent = []
+        p = here
+        self.zsem = {k: sems.take() for k in p.zs}
+        self.xsem = {(s, d): sems.take() for s in range(p.Z) for d in p.xs}
+        self.ysem = {(s, d): sems.take() for s in range(p.Z) for d in p.ys}
+        self.dsem = {
+            (s, h, dx, dy): sems.take()
+            for s in range(p.Z) for h in (0, 1) for dx in p.xs for dy in p.ys
+        }
+
+    def push(self, src, dst, sem, device):
+        copy = remote(src, dst, sem[0], sem[1], device)
+        copy.start()
+        self.sent.append(copy)
+
+    def arrive(self, place, sem):
+        remote(place, place, sem[0], sem[1], self.p.device(other=True)).wait_recv()
+
+    def spread_z(self):
+        p = self.p
+        for k in p.zs:
+            self.push(self.own, self.at(p.z, p.row, None), self.zsem[k], p.device(dz=-k))
+
+    def spread_xy(self, s):
+        p = self.p
+        zc = p.z_at(s)
+        place = self.at(zc, p.row, None)
+        src = self.own
+        if s:
+            self.arrive(place, self.zsem[s])
+            src = place
+        for d in p.xs:
+            self.push(src, place, self.xsem[s, d], p.device(dx=d))
+        for d in p.ys:
+            self.push(src, place, self.ysem[s, d], p.device(dy=d))
+
+    def spread_diagonal(self, s):
+        p = self.p
+        zc = p.z_at(s)
+        for d in p.xs:
+            r = p.row_at(dx=-d)
+            self.arrive(self.at(zc, r, None), self.xsem[s, d])
+            half = self.at(zc, r, 0)
+            for e in p.ys:
+                self.push(half, half, self.dsem[s, 0, d, e], p.device(dy=e))
+        for e in p.ys:
+            r = p.row_at(dy=-e)
+            self.arrive(self.at(zc, r, None), self.ysem[s, e])
+            half = self.at(zc, r, 1)
+            for d in p.xs:
+                self.push(half, half, self.dsem[s, 1, d, e], p.device(dx=d))
+
+    def close(self, s):
+        p = self.p
+        zc = p.z_at(s)
+        for d in p.xs:
+            for e in p.ys:
+                r = p.row_at(dy=-e, dx=-d)
+                for h in (0, 1):
+                    self.arrive(self.at(zc, r, h), self.dsem[s, h, d, e])
+
+    def finish(self):
+        for copy in self.sent:
+            copy.wait_send()
+
+
+def scatter_count(X, Y, Z):
+    return (Z - 1) + Z * (2 * (X - 1) * (Y - 1) + 2 * (X - 1) + 2 * (Y - 1))
+
+
+class Scatter:
+    def __init__(self, part, cut, here, sems, diag, fromx, fromy, sumx, sumy, sumz, fromz):
+        self.part, self.cut, self.p = part, cut, here
+        self.diag, self.fromx, self.fromy = diag, fromx, fromy
+        self.sumx, self.sumy, self.sumz, self.fromz = sumx, sumy, sumz, fromz
+        self.sent = []
+        p = here
+        self.zsem = {k: sems.take() for k in p.zs}
+        self.xsem = {(s, h, d): sems.take() for s in range(p.Z) for h in (0, 1) for d in p.xs}
+        self.ysem = {(s, h, d): sems.take() for s in range(p.Z) for h in (0, 1) for d in p.ys}
+        self.dsem = {
+            (s, h, dx, dy): sems.take()
+            for s in range(p.Z) for h in (0, 1) for dx in p.xs for dy in p.ys
+        }
+
+    def push(self, src, dst, sem, device):
+        copy = remote(src, dst, sem[0], sem[1], device)
+        copy.start()
+        self.sent.append(copy)
+
+    def arrive(self, place, sem):
+        remote(place, place, sem[0], sem[1], self.p.device(other=True)).wait_recv()
+
+    def spot(self, d, e):
+        return (d - 1) * (self.p.Y - 1) + e - 1
+
+    def first(self, s):
+        p, cut = self.p, self.cut
+        zc = p.z_at(s)
+        for d in p.xs:
+            for e in p.ys:
+                far = self.part(zc, p.row_at(dy=e, dx=d))
+                n = self.spot(d, e)
+                self.push(cut(far, 0), self.diag.at[s, 0, n], self.dsem[s, 0, d, e], p.device(dx=d))
+                self.push(cut(far, 1), self.diag.at[s, 1, n], self.dsem[s, 1, d, e], p.device(dy=e))
+        for d in p.xs:
+            near = self.part(zc, p.row_at(dx=d))
+            self.push(cut(near, 0), cut(self.fromx.at[s, d - 1], 0), self.xsem[s, 0, d], p.device(dx=d))
+        for e in p.ys:
+            near = self.part(zc, p.row_at(dy=e))
+            self.push(cut(near, 1), cut(self.fromy.at[s, e - 1], 1), self.ysem[s, 1, e], p.device(dy=e))
+
+    def second(self, s):
+        p, cut = self.p, self.cut
+        zc = p.z_at(s)
+        for e in p.ys:
+            total = cut(self.part(zc, p.row_at(dy=e)), 0)[...].astype(F32)
+            for d in p.xs:
+                place = self.diag.at[s, 0, self.spot(d, e)]
+                self.arrive(place, self.dsem[s, 0, d, e])
+                total = total + place[...].astype(F32)
+            self.sumy[s, e - 1] = total.astype(BF)
+            self.push(self.sumy.at[s, e - 1], cut(self.fromy.at[s, e - 1], 0), self.ysem[s, 0, e], p.device(dy=e))
+        for d in p.xs:
+            total = cut(self.part(zc, p.row_at(dx=d)), 1)[...].astype(F32)
+            for e in p.ys:
+                place = self.diag.at[s, 1, self.spot(d, e)]
+                self.arrive(place, self.dsem[s, 1, d, e])
+                total = total + place[...].astype(F32)
+            self.sumx[s, d - 1] = total.astype(BF)
+            self.push(self.sumx.at[s, d - 1], cut(self.fromx.at[s, d - 1], 1), self.xsem[s, 1, d], p.device(dx=d))
+
+    def third(self, s):
+        p, cut = self.p, self.cut
+        total = self.part(p.z_at(s), p.row)[...].astype(F32)
+        for d in p.xs:
+            for h in (0, 1):
+                self.arrive(cut(self.fromx.at[s, d - 1], h), self.xsem[s, h, d])
+            total = total + self.fromx[s, d - 1].astype(F32)
+        for e in p.ys:
+            for h in (0, 1):
+                self.arrive(cut(self.fromy.at[s, e - 1], h), self.ysem[s, h, e])
+            total = total + self.fromy[s, e - 1].astype(F32)
+        if s:
+            self.sumz[s - 1] = total.astype(BF)
+            self.push(self.sumz.at[s - 1], self.fromz.at[s - 1], self.zsem[s], p.device(dz=s))
+            return None
+        for k in p.zs:
+            self.arrive(self.fromz.at[k - 1], self.zsem[k])
+            total = total + self.fromz[k - 1].astype(F32)
+        return total
+
+    def finish(self):
+        for copy in self.sent:
+            copy.wait_send()
+
+
+def scatter_scratch(X, Y, Z, block, half):
+    return [
+        pltpu.VMEM((Z, 2, (X - 1) * (Y - 1)) + half, BF),
+        pltpu.VMEM((Z, X - 1) + block, BF),
+        pltpu.VMEM((Z, Y - 1) + block, BF),
+        pltpu.VMEM((Z, X - 1) + half, BF),
+        pltpu.VMEM((Z, Y - 1) + half, BF),
+        pltpu.VMEM((Z - 1,) + block, BF),
+        pltpu.VMEM((Z - 1,) + block, BF),
+    ]
+
+
+def sides(shape):
+    x = math.isqrt(shape[0])
+    while shape[0] % x:
+        x -= 1
+    return x, shape[0] // x, shape[1] // 2
+
+
+def gather_kernel(shape, with_slab, *refs):
+    if with_slab:
+        slab, ffn, slabs, ffns, asend, arecv, fsend, frecv, csend, crecv = refs
+    else:
+        ffn, ffns, fsend, frecv = refs
+    p = Place(shape)
+    p.greet()
+    br = ffn.shape[1]
+
+    def ffn_at(zc, r, half):
+        if half is None:
+            return ffns.at[zc, :, r]
+        return ffns.at[zc, :, r, pl.ds(half * (br // 2), br // 2)]
+
+    far = Gather(ffn_at, p, Sems(fsend, frecv), ffn)
+    ffns[p.z, :, p.row] = ffn[...]
+    if with_slab:
+        ar = slab.shape[0]
+
+        def slab_at(zc, r, half):
+            if half is None:
+                return slabs.at[r, zc, p.core]
+            return slabs.at[r, zc, p.core, pl.ds(half * (ar // 2), ar // 2)]
+
+        near = Gather(slab_at, p, Sems(asend, arecv), slab)
+        slabs[p.row, p.z, p.core] = slab[...]
+        mate = p.device(other=True)
+        passed = []
+
+        def hand(n, zc, r):
+            place = slabs.at[r, zc, p.core]
+            copy = remote(place, place, csend.at[n], crecv.at[n], mate)
+            copy.start()
+            passed.append((copy, zc, r, n))
+
+        near.spread_z()
+        near.spread_xy(0)
+        for s in range(p.Z):
+            if s + 1 < p.Z:
+                near.spread_xy(s + 1)
+            near.spread_diagonal(s)
+        far.spread_z()
+        far.spread_xy(0)
+        n = 0
+        for s in range(p.Z):
+            near.close(s)
+            zc = p.z_at(s)
+            for dy in range(p.Y):
+                for dx in range(p.X):
+                    hand(n, zc, p.row_at(dy, dx))
+                    n += 1
+        for copy, zc, r, n in passed:
+            copy.wait_send()
+            place = slabs.at[r, zc, 1 - p.core]
+            remote(place, place, csend.at[n], crecv.at[n], mate).wait_recv()
+        near.finish()
+    else:
+        far.spread_z()
+        far.spread_xy(0)
+    for s in range(p.Z):
+        if s + 1 < p.Z:
+            far.spread_xy(s + 1)
+        far.spread_diagonal(s)
+    for s in range(p.Z):
+        far.close(s)
+    far.finish()
+
+
+VM = pl.BlockSpec(memory_space=pltpu.VMEM)
+DMA = pltpu.SemaphoreType.DMA
+
+
+def gather_weights(shape, slab, ffn):
+    X, Y, Z = sides(shape)
+    R = shape[0]
+    n = gather_count(X, Y, Z)
+    with_slab = slab is not None
+    ffns = jax.ShapeDtypeStruct((Z, 3, R) + ffn.shape[1:], BF)
+    outs = [ffns]
+    args = [ffn]
+    scratch = [DMA((n,)), DMA((n,))]
+    if with_slab:
+        outs = [jax.ShapeDtypeStruct((R, Z, 2) + slab.shape, BF)] + outs
+        args = [slab] + args
+        scratch = [DMA((n,)), DMA((n,))] + scratch + [DMA((R * Z,)), DMA((R * Z,))]
+    return pl.pallas_call(
+        functools.partial(gather_kernel, shape, with_slab),
+        out_shape=outs,
+        in_specs=[VM] * len(args),
+        out_specs=[VM] * len(outs),
+        scratch_shapes=scratch,
+        compiler_params=pltpu.CompilerParams(
+            collective_id=0, has_side_effects=True, vmem_limit_bytes=48 << 20
+        ),
+        name="gather_weights",
+    )(*args)
+
+
+def scatter_kernel(shape, with_slab, *refs):
+    if with_slab:
+        slabs, ffns, slab_out, ffn_out = refs[:4]
+        scratch = refs[4:]
+        fwork, awork = scratch[:7], scratch[7:14]
+        plane, crossed, fsend, frecv, asend, arecv, csem = scratch[14:]
+    else:
+        ffns, ffn_out = refs[:2]
+        fwork = refs[2:9]
+        fsend, frecv = refs[9:]
+    p = Place(shape)
+    p.greet()
+    br = ffns.shape[3]
+
+    far = Scatter(
+        lambda zc, r: ffns.at[zc, :, r],
+        lambda ref, h: ref.at[:, pl.ds(h * (br // 2), br // 2)],
+        p, Sems(fsend, frecv), *fwork,
+    )
+    order = list(range(1, p.Z)) + [0]
+    if with_slab:
+        ar = slabs.shape[3]
+        cross = remote(
+            slabs.at[:, :, 1 - p.core], crossed, csem.at[0], csem.at[1], p.device(other=True)
+        )
+        cross.start()
+    for s in order:
+        far.first(s)
+    if with_slab:
+        cross.wait()
+
+        def fold(n, carry):
+            r, zc = n // p.Z, n % p.Z
+            mine = slabs[r, zc, p.core].astype(F32) + crossed[r, zc].astype(F32)
+            plane[r, zc] = mine.astype(BF)
+            return carry
+
+        lax.fori_loop(0, p.R * p.Z, fold, 0)
+        near = Scatter(
+            lambda zc, r: plane.at[r, zc],
+            lambda ref, h: ref.at[pl.ds(h * (ar // 2), ar // 2)],
+            p, Sems(asend, arecv), *awork,
+        )
+        for s in order:
+            near.first(s)
+    for s in order:
+        far.second(s)
+    if with_slab:
+        for s in order:
+            near.second(s)
+    for s in order:
+        total = far.third(s)
+    ffn_out[...] = total
+    if with_slab:
+        for s in order:
+            total = near.third(s)
+        slab_out[...] = total
+        near.finish()
+    far.finish()
+
+
+def scatter_grads(shape, slabs, ffns):
+    X, Y, Z = sides(shape)
+    R = shape[0]
+    n = scatter_count(X, Y, Z)
+    with_slab = slabs is not None
+    block = (3,) + ffns.shape[3:]
+    half = (3, ffns.shape[3] // 2, ffns.shape[4])
+    outs = [jax.ShapeDtypeStruct(block, F32)]
+    args = [ffns]
+    scratch = scatter_scratch(X, Y, Z, block, half)
+    if with_slab:
+        ablock = slabs.shape[3:]
+        ahalf = (ablock[0] // 2, ablock[1])
+        outs = [jax.ShapeDtypeStruct(ablock, F32)] + outs
+        args = [slabs] + args
+        scratch += scatter_scratch(X, Y, Z, ablock, ahalf)
+        scratch += [pltpu.VMEM((R, Z) + ablock, BF)] * 2
+    scratch += [DMA((n,)), DMA((n,))]
+    if with_slab:
+        scratch += [DMA((n,)), DMA((n,)), DMA((2,))]
+    return pl.pallas_call(
+        functools.partial(scatter_kernel, shape, with_slab),
+        out_shape=outs,
+        in_specs=[VM] * len(args),
+        out_specs=[VM] * len(outs),
+        scratch_shapes=scratch,
+        compiler_params=pltpu.CompilerParams(
+            collective_id=1, has_side_effects=True, vmem_limit_bytes=60 << 20
+        ),
+        name="scatter_grads",
+    )(*args)
 
 
 def from_behind(block, axis, distance):
@@ -20,20 +469,8 @@
     return lax.ppermute(block, axis, route)
 
 
-def product(left, right):
-    return jnp.dot(left, right, preferred_element_type=jnp.float32)
-
-
-def inner(left, right):
-    return lax.dot_general(
-        left, right, (((0,), (0,)), ((), ())), preferred_element_type=jnp.float32
-    )
-
-
-def against(left, right):
-    return lax.dot_general(
-        left, right, (((1,), (1,)), ((), ())), preferred_element_type=jnp.float32
-    )
+def swap(block):
+    return lax.ppermute(block, "col", [(i, i ^ 1) for i in range(lax.axis_size("col"))])
 
 
 def gated(gate, up):
@@ -47,17 +484,31 @@
 
 
 def shards(
+    shape,
     tokens, gain_attn, w_query, w_keyval, w_out, gain_mlp, w_gate, w_up, w_down, segment, cotangent
 ):
-    gain_first, gain_second, query_weight, keyval_weight, out_weight = (
-        lax.all_gather(gain_attn, ("row", "col"), axis=0, tiled=True),
-        lax.all_gather(gain_mlp, ("row", "col"), axis=0, tiled=True),
-        lax.all_gather(w_query, ("row", "col"), axis=0, tiled=True),
-        lax.all_gather(w_keyval, ("row", "col"), axis=0, tiled=True),
-        lax.all_gather(w_out, ("row", "col"), axis=0, tiled=True),
-    )
-    gain_first = gain_first.astype(jnp.float32)
-    gain_second = gain_second.astype(jnp.float32)
+    R, C = shape
+    D = tokens.shape[1]
+    with_slab = w_query.shape[0] % 32 == 0
+    ffn = jnp.stack([w_gate, w_up, w_down.T])
+    slab = jnp.concatenate(
+        [w_query, w_keyval, w_out,
+         jnp.pad(jnp.stack([gain_attn, gain_mlp], axis=1), ((0, 0), (0, 126)))], axis=1)
+    if with_slab:
+        slabs, ffns = gather_weights(shape, slab, ffn)
+        slabs = slabs.reshape(D, slab.shape[1])
+    else:
+        slabs = lax.all_gather(slab, ("row", "col"), axis=0, tiled=True)
+        (ffns,) = gather_weights(shape, None, ffn)
+    E = H * DH
+    query_weight = slabs[:, :E]
+    keyval_weight = slabs[:, E : E + 2 * DH]
+    out_weight = slabs[:, E + 2 * DH : 2 * E + 2 * DH]
+    gain_first = slabs[:, 2 * E + 2 * DH].astype(F32)
+    gain_second = slabs[:, 2 * E + 2 * DH + 1].astype(F32)
+    Z = C // 2
+    ffns = ffns.reshape(Z, 3, D, -1)
+
     rows = tokens.shape[0]
     inputs = tokens.astype(jnp.float32)
     scale_first = lax.rsqrt(jnp.mean(inputs * inputs, axis=-1, keepdims=True) + EPS)
@@ -107,46 +558,32 @@
     scale_second = lax.rsqrt(jnp.mean(middle * middle, axis=-1, keepdims=True) + EPS)
     normed_second = middle * scale_second
     mlp_in = (normed_second * gain_second).astype(jnp.bfloat16)
-    gate_weight, up_weight, down_weight = (
-        lax.all_gather(w_gate, "row", axis=0, tiled=True),
-        lax.all_gather(w_up, "row", axis=0, tiled=True),
-        lax.all_gather(w_down, "row", axis=1, tiled=True),
-    )
-    piece = lax.all_gather(mlp_in, "col", axis=0, tiled=True)
-    hidden = gated(product(piece, gate_weight), product(piece, up_weight)).astype(jnp.bfloat16)
-    mlp_out = lax.psum_scatter(
-        product(hidden, down_weight).astype(jnp.bfloat16), "col", scatter_dimension=0, tiled=True
-    ).astype(jnp.float32)
+
+    other_in = swap(mlp_in)
+    other_grad = swap(cotangent)
+    both_in = jnp.concatenate([mlp_in, other_in])
+    both_grad = jnp.concatenate([cotangent, other_grad])
+    out_sum = 0.0
+    grad_in_sum = 0.0
+    weight_grads = []
+    for zc in range(Z):
+        gate_w, up_w, down_w = ffns[zc, 0], ffns[zc, 1], ffns[zc, 2]
+        gate_rows, up_rows = product(both_in, gate_w), product(both_in, up_w)
+        grad_hidden = product(both_grad, down_w)
+        hidden, pull = jax.vjp(gated, gate_rows, up_rows)
+        hidden = hidden.astype(BF)
+        grad_gate, grad_up = pull(grad_hidden)
+        grad_gate, grad_up = grad_gate.astype(BF), grad_up.astype(BF)
+        out_sum += against(hidden, down_w)
+        grad_in_sum += against(grad_gate, gate_w) + against(grad_up, up_w)
+        weight_grads.append(
+            jnp.stack([inner(both_in, grad_gate), inner(both_in, grad_up), inner(both_grad, hidden)]).astype(BF)
+        )
+    weight_grads = jnp.stack(weight_grads).reshape((Z, 3, R) + w_gate.shape)
+    mlp_out = out_sum[:rows] + swap(out_sum[rows:].astype(BF)).astype(F32)
+    grad_mlp_in = grad_in_sum[:rows] + swap(grad_in_sum[rows:])
     output = (middle + mlp_out).astype(jnp.bfloat16)
-    inputs_piece = lax.all_gather(mlp_in, "col", axis=0, tiled=True)
-    grad_piece = lax.all_gather(cotangent, "col", axis=0, tiled=True)
-    gate_rows = product(inputs_piece, gate_weight)
-    up_rows = product(inputs_piece, up_weight)
-    grad_hidden = against(grad_piece, down_weight)
-    _, pull = jax.vjp(gated, gate_rows, up_rows)
-    grad_gate, grad_up = pull(grad_hidden)
-    grad_gate = grad_gate.astype(jnp.bfloat16)
-    grad_up = grad_up.astype(jnp.bfloat16)
-    gate_grad = inner(inputs_piece, grad_gate)
-    up_grad = inner(inputs_piece, grad_up)
-    down_grad = inner(hidden, grad_piece)
-    grad_mlp_in = lax.psum_scatter(
-        against(grad_gate, gate_weight) + against(grad_up, up_weight),
-        "col",
-        scatter_dimension=0,
-        tiled=True,
-    )
-    gate_grad, up_grad, down_grad = (
-        lax.psum_scatter(
-            gate_grad.astype(jnp.bfloat16), "row", scatter_dimension=0, tiled=True
-        ).astype(jnp.float32),
-        lax.psum_scatter(
-            up_grad.astype(jnp.bfloat16), "row", scatter_dimension=0, tiled=True
-        ).astype(jnp.float32),
-        lax.psum_scatter(
-            down_grad.astype(jnp.bfloat16), "row", scatter_dimension=1, tiled=True
-        ).astype(jnp.float32),
-    )
+
     grad_outputs = cotangent.astype(jnp.float32)
     gain_second_grad = jnp.sum(grad_mlp_in * normed_second, axis=0)
     grad_middle = grad_outputs + norm_back(grad_mlp_in * gain_second, middle, scale_second)
@@ -194,30 +631,34 @@
     keyval_grad = inner(attn_in, grad_keyval_act)
     gain_first_grad = jnp.sum(grad_attn_in * normed_first, axis=0)
     grad_inputs = grad_middle + norm_back(grad_attn_in * gain_first, inputs, scale_first)
-    gain_first_grad, gain_second_grad, query_grad, keyval_grad, out_grad = (
-        lax.psum_scatter(gain_first_grad, ("row", "col"), scatter_dimension=0, tiled=True),
-        lax.psum_scatter(gain_second_grad, ("row", "col"), scatter_dimension=0, tiled=True),
-        lax.psum_scatter(query_grad, ("row", "col"), scatter_dimension=0, tiled=True),
-        lax.psum_scatter(keyval_grad, ("row", "col"), scatter_dimension=0, tiled=True),
-        lax.psum_scatter(out_grad, ("row", "col"), scatter_dimension=0, tiled=True),
-    )
+
+    gains = jnp.pad(jnp.stack([gain_first_grad, gain_second_grad], axis=1), ((0, 0), (0, 126)))
+    slab_grads = jnp.concatenate([query_grad, keyval_grad, out_grad, gains], axis=1)
+    if with_slab:
+        slab_grad, ffn_grad = scatter_grads(
+            shape, slab_grads.astype(BF).reshape((R, Z, 2) + slab.shape), weight_grads
+        )
+    else:
+        slab_grad = lax.psum_scatter(slab_grads, ("row", "col"), scatter_dimension=0, tiled=True)
+        (ffn_grad,) = scatter_grads(shape, None, weight_grads)
     return (
         output,
         grad_inputs,
-        gain_first_grad,
-        query_grad,
-        keyval_grad,
-        out_grad,
-        gain_second_grad,
-        gate_grad,
-        up_grad,
-        down_grad,
+        slab_grad[:, 2 * E + 2 * DH],
+        slab_grad[:, :E],
+        slab_grad[:, E : E + 2 * DH],
+        slab_grad[:, E + 2 * DH : 2 * E + 2 * DH],
+        slab_grad[:, 2 * E + 2 * DH + 1],
+        ffn_grad[0],
+        ffn_grad[1],
+        ffn_grad[2].T,
     )
 
 
 def solution(mesh):
+    shape = (mesh.shape["row"], mesh.shape["col"])
     return jax.shard_map(
-        shards,
+        functools.partial(shards, shape),
         mesh=mesh,
         in_specs=(
             P(("row", "col"), None),

time: 1160 us -> 609 us (0.53)
  the two profiles are of different devices: /device:TPU:0 before, /device:TPU:17 now
where the time goes in v1:
time: 609 us; the launch traced here: 600 us
  Pallas kernels  258 us (42%)
  matrix products  210 us (34%)
  other arithmetic  51.8 us (9%)
  local copies, waits for them, and re-layouts  44.5 us (7%)
  starting transfers between devices  30.5 us (5%)
    pallas_call x1, Pallas kernels, scatter_grads(): pl.pallas_call(functools.partial(scatter_kernel, shape, with_slab), out_s...  158 us
    pallas_call x1, Pallas kernels, gather_weights(): pl.pallas_call(functools.partial(gather_kernel, shape, with_slab), out_sh...  100 us
    dot_general x15, matrix products, against(): lax.dot_general(left, right, (((1,), (1,)), ((), ())), preferred_element_...  49.5 us
    dot_general x15, matrix products, product(): return jnp.dot(left, right, preferred_element_type=jnp.float32)  43.8 us
    dot_general x15, matrix products, inner(): lax.dot_general(left, right, (((0,), (0,)), ((), ())), preferred_element_...  38.9 us
    ppermute x6, starting transfers between devices, from_behind(): return lax.ppermute(block, axis, route)  29.1 us
    dot_general x8, matrix products, scores_of(): jnp.einsum('gqd,kd->gqk', part, keys, preferred_element_type=jnp.float32)  22.1 us
    dot_general x4, matrix products, backward_group(): jnp.einsum('gqk,gqd->kd', probs.astype(jnp.bfloat16), grad_part, preferre...  19.4 us
  transfers between devices with their start and end apart: 10, of which 2 were waited for; matrix products, arithmetic and copies ran while one was open for 15% of the time, Pallas kernels for 0%

profile of v1, /device:TPU:17, one launch (start us, length us, event | category | flops | bytes accessed | tf_op | source)
XLA Modules:
  0.0 599.6 jit_solution(1079796508662244811)
XLA Ops:
  4.6 100.0 %gather_weights.1 = (bf16[4,4,2,32,2432]{4,3,2,1,0:T(8,128)(2,1)S(1)}, bf16[4,3,4,256,384]{4,3,2,1,0:T(8,128)(2,1)}) custom-call(bf16[32,2432]{1,0:T(8,128)(2,1)S(1)} %fusion.142.refs_0_, bf16[3,256,384]{2,1,0:T(8,128)(2,1)S(1)} %pad_maximum_fusion.4.refs_1_), custom_call_target="tpu_custom_call" | custom-call | tf_op jit(solution)/shard_map/gather_weights/pallas_call | solution.py:359
  109.6 10.9 %collective-permute-start.3 = (bf16[512,256]{1,0:T(8,128)(2,1)S(1)}, bf16[512,256]{1,0:T(8,128)(2,1)}, u32[]{:S(2)}, u32[]{:S(2)}) collective-permute-start(bf16[512,256]{1,0:T(8,128)(2,1)S(1)} %convolution_convert_fusion.15), channel_id=1, source_target_pairs={{0,1},{1,2},{2,3},{3,4},{4,5},{5,6},{6,7},{8,9},{9,10},{10,11},{11... | collective-permute-start | bytes 786440 | tf_op jit(solution)/shard_map/ppermute | solution.py:469
  126.9 3.9 fusion.104
  134.0 34.2 %while.28 = (s32[]{:T(128)}, bf16[4,2,512,128]{2,3,1,0:T(8,128)(2,1)}, f32[4,2,512,1]{2,1,3,0:T(2,128)S(1)}, bf16[4,2,512,128]{3,2,1,0:T(8,128)(2,1)S(1)}, bf16[...) while((s32[]{:T(128)}, ...), condition=%wide.region_4.5_spmd.clone, body=%wide.region_1.4_spmd.clone.sunk | while | flops 832175104 | bytes 24422520 | solution.py:555
  169.4 3.5 multiply_reduce_fusion.3
  177.1 3.4 fusion.124
  183.7 3.5 multiply_convert_fusion.3
  225.4 3.5 multiply_convert_fusion.2
  244.2 9.6 %add_add_fusion = f32[1024,1024]{1,0:T(8,128)} fusion(f32[1024,1024]{1,0:T(8,128)S(1)} %fusion.129, f32[1024,1024]{1,0:T(8,128)S(1)} %fusion.123, f32[1024,1024]{1,0:T(8,128)S(1)} %fusion.125, f32[1024,1024]{1,0:T(8,128)S(1)} %fusion.117, f32[1024,1024]{1,0:T(8,128)} %fusion.119, f32[1024,1024]{1,0:T(8,128)} %fusion.111, f32[1024,1024]{1,0:T(8,128)} %fusion.113, ...), kind=kOutput, calls=%fused_computation.64 | convolution fusion | flops 812646400 | bytes 35127296 | tf_op jit(solution)/shard_map/dot_general | solution.py:33
  259.6 4.0 add_add_fusion.1
  288.5 6.7 %maximum_maximum_fusion.refs_1_ = bf16[4,3,4,256,384]{4,3,2,1,0:T(8,128)(2,1)} fusion(bf16[1,1,4,256,384]{4,3,2,1,0:T(8,128)(2,1)S(1)} %bitcast.294, bf16[1,1,4,256,384]{4,3,2,1,0:T(8,128)(2,1)S(1)} %bitcast.295, bf16[1,1,4,256,384]{4,3,2,1,0:T(8,128)(2,1)S(1)} %bitcast.296, bf16[1,1,4,256,384]{4,3,2,1,0:T(8,128)(2,1)S(1)} %bitcast.291, ...), kind=kLoop, calls=%fused_computation.62 | loop fusion | flops 51904512 | bytes 18874368 | tf_op jit(solution)/shard_map/stack | solution.py:582
  304.5 85.7 %while.29 = (s32[]{:T(128)}, bf16[4,2,512,128]{2,3,1,0:T(8,128)(2,1)}, f32[4,1536,128]{2,1,0:T(8,128)}, f32[4,1536,128]{2,1,0:T(8,128)}, bf16[4,2,512,128]{3,2,1...) while((s32[]{:T(128)}, ...), condition=%wide.region_9.10_spmd.clone, body=%wide.region_7.9_spmd.clone.sunk | while | flops 2034170880 | bytes 92176720 | solution.py:615
  307.2 3.9 multiply_reduce_fusion.5
  321.2 4.9 fusion.226
  328.6 3.9 multiply_reduce_fusion.5
  342.6 4.9 fusion.226
  350.0 3.9 multiply_reduce_fusion.5
  364.0 4.8 fusion.226
  371.4 4.0 multiply_reduce_fusion.5
  385.4 4.8 fusion.226
  390.2 4.6 fusion.69
  401.7 9.6 %collective-permute-start.9 = (bf16[512,256]{1,0:T(8,128)(2,1)S(1)}, bf16[512,256]{1,0:T(8,128)(2,1)S(1)}, u32[]{:S(2)}, u32[]{:S(2)}) collective-permute-start(bf16[512,256]{1,0:T(8,128)(2,1)S(1)} %get-tuple-element.271), channel_id=1, source_target_pairs={{2,0},{3,1},{4,2},{5,3},{6,4},{7,5},{10,8},{11,9},{12,10},{13,11},... | collective-permute-start | bytes 786440 | tf_op jit(solution)/shard_map/ppermute | solution.py:469
  424.2 4.0 fusion.144
  434.0 157.6 %scatter_grads.1 = (f32[32,2432]{1,0:T(8,128)}, f32[3,256,384]{2,1,0:T(8,128)}) custom-call(bf16[4,4,2,32,2432]{4,3,2,1,0:T(8,128)(2,1)} %pad_maximum_fusion.refs_0_, bf16[4,3,4,256,384]{4,3,2,1,0:T(8,128)(2,1)} %maximum_maximum_fusion.refs_1_), custom_call_target="tpu_custom_call" | custom-call | tf_op jit(solution)/shard_map/scatter_grads/pallas_call | solution.py:453
  (311 shorter events, 236.6 us)
Async XLA Ops:
  2.5 104.7 %copy-start.9 = (bf16[512,1024]{1,0:T(8,128)(2,1)S(1)}, bf16[512,1024]{1,0:T(8,128)(2,1)}, u32[]{:S(2)}) copy-start(bf16[512,1024]{1,0:T(8,128)(2,1)} %param.15) | copy-start | bytes 3145732
  107.2 19.7 %copy-start.43 = (f32[1024,1]{0,1:T(1,128)}, f32[1024,1]{0,1:T(1,128)S(1)}, u32[]{:S(2)}) copy-start(f32[1024,1]{0,1:T(1,128)S(1)} %copy.81) | copy-start | bytes 12292
  107.2 15.2 %copy-start.48 = (s32[512]{0:T(512)S(1)}, s32[512]{0:T(512)}, u32[]{:S(2)}) copy-start(s32[512]{0:T(512)} %param.24) | copy-start | bytes 6148
  108.1 22.6 %copy-start.45 = (f32[512]{0:T(512)}, f32[512]{0:T(512)S(1)}, u32[]{:S(2)}) copy-start(f32[512]{0:T(512)S(1)} %get-tuple-element.277) | copy-start | bytes 6148
  109.6 23.3 %collective-permute-start.3 = (bf16[512,256]{1,0:T(8,128)(2,1)S(1)}, bf16[512,256]{1,0:T(8,128)(2,1)}, u32[]{:S(2)}, u32[]{:S(2)}) collective-permute-start(bf16[512,256]{1,0:T(8,128)(2,1)S(1)} %convolution_convert_fusion.15), channel_id=1, source_target_pairs={{0,1},{1,2},{2,3},{3,4},{4,5},{5,6},{6,7},{8,9},{9,10},{10,11},{11... | collective-permute-start | bytes 786440 | tf_op jit(solution)/shard_map/ppermute | solution.py:469
  120.5 12.4 %collective-permute-start.2 = (bf16[512,256]{1,0:T(8,128)(2,1)S(1)}, bf16[512,256]{1,0:T(8,128)(2,1)}, u32[]{:S(2)}, u32[]{:S(2)}) collective-permute-start(bf16[512,256]{1,0:T(8,128)(2,1)S(1)} %convolution_convert_fusion.15), channel_id=1, source_target_pairs={{0,2},{1,3},{2,4},{3,5},{4,6},{5,7},{8,10},{9,11},{10,12},{11,13},... | collective-permute-start | bytes 786440 | tf_op jit(solution)/shard_map/ppermute | solution.py:469
  122.4 10.4 %collective-permute-start.1 = (s32[512]{0:T(512)S(1)}, s32[512]{0:T(512)S(1)}, u32[]{:S(2)}, u32[]{:S(2)}) collective-permute-start(s32[512]{0:T(512)S(1)} %broadcast_add_fusion), channel_id=1, source_target_pairs={{0,1},{1,2},{2,3},{3,4},{4,5},{5,6},{6,7},{8,9},{9,10},{10,11},{11... | collective-permute-start | bytes 6152 | tf_op jit(solution)/shard_map/ppermute | solution.py:469
  124.4 8.5 %collective-permute-start = (s32[512]{0:T(512)S(1)}, s32[512]{0:T(512)S(1)}, u32[]{:S(2)}, u32[]{:S(2)}) collective-permute-start(s32[512]{0:T(512)S(1)} %broadcast_add_fusion), channel_id=1, source_target_pairs={{0,2},{1,3},{2,4},{3,5},{4,6},{5,7},{8,10},{9,11},{10,12},{11,13},... | collective-permute-start | bytes 6152 | tf_op jit(solution)/shard_map/ppermute | solution.py:469
  126.3 49.2 %collective-permute-start.6 = (bf16[512,1024]{1,0:T(8,128)(2,1)}, bf16[512,1024]{1,0:T(8,128)(2,1)}, u32[]{:S(2)}, u32[]{:S(2)}) collective-permute-start(bf16[512,1024]{1,0:T(8,128)(2,1)} %param.25), channel_id=1, source_target_pairs={{0,1},{1,0},{2,3},{3,2},{4,5},{5,4},{6,7},{7,6},{8,9},{9,8},{10,11... | collective-permute-start | bytes 3145736 | tf_op jit(solution)/shard_map/ppermute | solution.py:473
  174.1 3.0 collective-permute-start.4
  176.8 48.6 %copy-start.39 = (bf16[1024,1024]{1,0:T(8,128)(2,1)}, bf16[1024,1024]{1,0:T(8,128)(2,1)S(1)}, u32[]{:S(2)}) copy-start(bf16[1024,1024]{1,0:T(8,128)(2,1)S(1)} %constant_dynamic-update-slice_fusion.2) | copy-start | bytes 6291460
  177.1 10.2 %slice-start = ((s8[9437184]{0:T(1024)(128)(4,1)}), s8[4194304]{0:T(1024)(128)(4,1)S(1)}, s32[]{:S(2)}) async-start(s8[9437184]{0:T(1024)(128)(4,1)} %bitcast.267), calls=%async_computation | async-start | bytes 8388608
  187.3 42.9 %copy-start.17 = (bf16[1024,384]{1,0:T(8,128)(2,1)}, bf16[1024,384]{1,0:T(8,128)(2,1)S(1)}, u32[]{:S(2)}) copy-start(bf16[1024,384]{1,0:T(8,128)(2,1)S(1)} %get-tuple-element.261) | copy-start | bytes 2359300
  187.3 44.2 %copy-start.19 = (bf16[1024,384]{1,0:T(8,128)(2,1)}, bf16[1024,384]{1,0:T(8,128)(2,1)S(1)}, u32[]{:S(2)}) copy-start(bf16[1024,384]{1,0:T(8,128)(2,1)S(1)} %get-tuple-element.260) | copy-start | bytes 2359300
  200.7 32.1 %copy-start.21 = (bf16[1024,384]{1,0:T(8,128)(2,1)}, bf16[1024,384]{1,0:T(8,128)(2,1)S(1)}, u32[]{:S(2)}) copy-start(bf16[1024,384]{1,0:T(8,128)(2,1)S(1)} %get-tuple-element.258) | copy-start | bytes 2359300
  200.7 33.8 %copy-start.23 = (bf16[1024,384]{1,0:T(8,128)(2,1)}, bf16[1024,384]{1,0:T(8,128)(2,1)S(1)}, u32[]{:S(2)}) copy-start(bf16[1024,384]{1,0:T(8,128)(2,1)S(1)} %get-tuple-element.257) | copy-start | bytes 2359300
  214.3 23.5 %copy-start.25 = (bf16[1024,384]{1,0:T(8,128)(2,1)}, bf16[1024,384]{1,0:T(8,128)(2,1)S(1)}, u32[]{:S(2)}) copy-start(bf16[1024,384]{1,0:T(8,128)(2,1)S(1)} %get-tuple-element.255) | copy-start | bytes 2359300
  214.3 26.7 %copy-start.27 = (bf16[1024,384]{1,0:T(8,128)(2,1)}, bf16[1024,384]{1,0:T(8,128)(2,1)S(1)}, u32[]{:S(2)}) copy-start(bf16[1024,384]{1,0:T(8,128)(2,1)S(1)} %get-tuple-element.254) | copy-start | bytes 2359300
  255.8 39.5 %collective-permute-start.7 = (f32[512,1024]{1,0:T(8,128)S(1)}, f32[512,1024]{1,0:T(8,128)S(1)}, u32[]{:S(2)}, u32[]{:S(2)}) collective-permute-start(f32[512,1024]{1,0:T(8,128)S(1)} %slice.161), channel_id=1, source_target_pairs={{0,1},{1,0},{2,3},{3,2},{4,5},{5,4},{6,7},{7,6},{8,9},{9,8},{10,11... | collective-permute-start | bytes 6291464 | tf_op jit(solution)/shard_map/ppermute | solution.py:473
  263.9 32.2 %collective-permute-start.5 = (bf16[512,1024]{1,0:T(8,128)(2,1)S(1)}, bf16[512,1024]{1,0:T(8,128)(2,1)S(1)}, u32[]{:S(2)}, u32[]{:S(2)}) collective-permute-start(bf16[512,1024]{1,0:T(8,128)(2,1)S(1)} %slice.252), channel_id=1, source_target_pairs={{0,1},{1,0},{2,3},{3,2},{4,5},{5,4},{6,7},{7,6},{8,9},{9,8},{10,11... | collective-permute-start | bytes 3145736 | tf_op jit(solution)/shard_map/ppermute | solution.py:473
  400.3 13.9 %copy-start.12 = (f32[512,1024]{1,0:T(8,128)S(1)}, f32[512,1024]{1,0:T(8,128)}, u32[]{:S(2)}) copy-start(f32[512,1024]{1,0:T(8,128)} %copy-done.11) | copy-start | bytes 6291460
  400.3 13.9 %copy-start.50 = (bf16[4,2,512,128]{2,3,1,0:T(8,128)(2,1)S(1)}, bf16[4,2,512,128]{2,3,1,0:T(8,128)(2,1)}, u32[]{:S(2)}) copy-start(bf16[4,2,512,128]{2,3,1,0:T(8,128)(2,1)} %get-tuple-element.107) | copy-start | bytes 3145732
  401.7 15.2 %collective-permute-start.9 = (bf16[512,256]{1,0:T(8,128)(2,1)S(1)}, bf16[512,256]{1,0:T(8,128)(2,1)S(1)}, u32[]{:S(2)}, u32[]{:S(2)}) collective-permute-start(bf16[512,256]{1,0:T(8,128)(2,1)S(1)} %get-tuple-element.271), channel_id=1, source_target_pairs={{2,0},{3,1},{4,2},{5,3},{6,4},{7,5},{10,8},{11,9},{12,10},{13,11},... | collective-permute-start | bytes 786440 | tf_op jit(solution)/shard_map/ppermute | solution.py:469
  411.3 7.7 %collective-permute-start.8 = (bf16[512,256]{1,0:T(8,128)(2,1)S(1)}, bf16[512,256]{1,0:T(8,128)(2,1)S(1)}, u32[]{:S(2)}, u32[]{:S(2)}) collective-permute-start(bf16[512,256]{1,0:T(8,128)(2,1)S(1)} %get-tuple-element.270), channel_id=1, source_target_pairs={{1,0},{2,1},{3,2},{4,3},{5,4},{6,5},{7,6},{9,8},{10,9},{11,10},{12... | collective-permute-start | bytes 786440 | tf_op jit(solution)/shard_map/ppermute | solution.py:469
  (58 other events, 178.0 us)
